TPU v7x, 512 devices: a whole 4x8x8 slice. The times are simulated.
512 devices in a mesh: row: 16 (over y, core), col: 32 (over x, z).
Axes of the slice: x: 4, y: 8, z: 8, core: 2. Of those that a mesh axis runs over, the one named last changes fastest.
Arguments:
- hidden_acts: bfloat16 [256, 29568], P('row', 'col'), may hold values from -6 to 6
- output_errors: bfloat16 [256, 4096], P('col', 'row'), may hold values from -6 to 6
- col_points: int32 [32], replicated, may hold values from 0 to 64, as said below
- row_points: int32 [16], replicated, may hold values from 0 to 32, as said below
- worker_mask: int32 [16, 32], replicated, may hold values from 0 to 1, as said below
Outputs:
- clipped_grad: float32 [8, 512, 29568], P(None, 'col', 'row')
Inputs may be any that keep to these rules, and one draw needn't show every extreme that they name: `col_points`: distinct node indices. `row_points`: distinct node indices. `worker_mask`: each row of the grid has between 1 and 8 erased workers.
All inputs are finite; a program needn't handle non-finite values.
Results may differ from a plain program's by a relative error of at most 0.02.
Values may be sent and summed in bfloat16 or wider, within the bound.
No kernel may reach another device: no remote copies, remote signals or barrier semaphores. Data moves between devices by JAX's collectives and lax.ppermute only.
A program may use at most 128 MiB of HBM per device.

v0:
```python
import jax
import jax.numpy as jnp
from jax import lax
from jax.sharding import Mesh
from jax.sharding import PartitionSpec as P

D = 4096
FF = 29568
COL = ("col_0", "col_1")
ROW = ("row_0", "row_1")
ROW_COL = ("row_0", "row_1", "col_0", "col_1")


def copy_for_each(shard, axis):
    peers = lax.axis_size(axis)
    return lax.all_to_all(
        jnp.broadcast_to(shard[None], (peers, *shard.shape)), axis, 0, 0, tiled=True
    )


def laid_out(blocks, dim):
    lengths = list(blocks.shape[1:])
    lengths[dim] *= blocks.shape[0]
    return jnp.moveaxis(blocks, 0, dim).reshape(lengths)


def gathered_copies(shard, axis, dim):
    blocks = copy_for_each(shard, axis)
    return laid_out(blocks, dim)


def one_axis_at_a_time(shard, axes):
    for axis in axes:
        shard = lax.psum(shard, axis)
    return shard


def node_value(index, count):
    return jnp.cos(jnp.pi * (2.0 * index.astype(jnp.float32) + 1.0) / (2.0 * count))


def berrut(nodes, signs, live, targets):
    terms = (live * signs)[:, None] / (targets[None, :] - nodes[:, None])
    return terms / jnp.sum(terms, axis=0, keepdims=True)


def rank_signs(points, live):
    lower = (points[None, :] < points[:, None]).astype(jnp.int32)
    ranks = jnp.sum(lower * live[None, :], axis=1)
    return (1 - 2 * (ranks % 2)).astype(jnp.float32)


def encode_blocks(source, weights, block_count, block_width):

    def add_block(index, total):
        piece = lax.dynamic_slice_in_dim(source, index * block_width, block_width, 1).astype(
            jnp.float32
        )
        factor = lax.dynamic_slice_in_dim(weights, index, 1, 0)
        return total + factor * piece

    start = jnp.zeros((source.shape[0], block_width), jnp.float32)
    return lax.fori_loop(0, block_count, add_block, start).astype(jnp.bfloat16)


def shards(hidden_acts, output_errors, col_points, row_points, worker_mask):
    col_count = lax.axis_size(COL)
    row_count = lax.axis_size(ROW)
    col_place = lax.axis_index(COL)
    row_place = lax.axis_index(ROW)
    act_blocks = col_count // 2
    err_blocks = row_count // 2
    act_width = FF // act_blocks
    err_width = D // err_blocks
    data_acts = node_value(jnp.arange(act_blocks), act_blocks)
    data_errs = node_value(jnp.arange(err_blocks), err_blocks)
    work_acts = node_value(col_points, 2 * col_count + 1)
    work_errs = node_value(row_points, 2 * row_count + 1)
    alt_acts = (1 - 2 * (jnp.arange(act_blocks) % 2)).astype(jnp.float32)
    alt_errs = (1 - 2 * (jnp.arange(err_blocks) % 2)).astype(jnp.float32)
    full_acts = gathered_copies(hidden_acts, COL, 1)
    own_node = lax.dynamic_slice_in_dim(work_acts, col_place, 1, 0)
    encode_own = berrut(data_acts, alt_acts, jnp.ones((act_blocks,), jnp.float32), own_node)[:, 0]
    coded_acts = encode_blocks(full_acts, encode_own, act_blocks, act_width)
    full_errs = lax.all_gather(output_errors, ROW, axis=1, tiled=True)
    own_err = lax.dynamic_slice_in_dim(work_errs, row_place, 1, 0)
    encode_err = berrut(data_errs, alt_errs, jnp.ones((err_blocks,), jnp.float32), own_err)[:, 0]
    coded_errs = encode_blocks(full_errs, encode_err, err_blocks, err_width)
    all_errs = gathered_copies(coded_errs, COL, 0)
    product = lax.dot_general(
        all_errs,
        lax.all_gather(coded_acts, ROW, axis=0, tiled=True),
        (((0,), (0,)), ((), ())),
        preferred_element_type=jnp.float32,
    ).astype(jnp.bfloat16)
    live = lax.dynamic_slice_in_dim(worker_mask, row_place, 1, 0)[0]
    decode_acts = berrut(
        work_acts, rank_signs(col_points, live), live.astype(jnp.float32), data_acts
    )
    decoded = jnp.einsum(
        "jk,jrf->rkf",
        decode_acts,
        lax.all_to_all(product[None], COL, split_axis=1, concat_axis=0, tiled=True).astype(
            jnp.float32
        ),
    ).astype(jnp.bfloat16)
    decoded = decoded.reshape(decoded.shape[0], FF)
    all_rows = jnp.ones((row_count,), jnp.int32)
    decode_errs = berrut(
        work_errs, rank_signs(row_points, all_rows), jnp.ones((row_count,), jnp.float32), data_errs
    )
    grad = jnp.einsum(
        "il,irf->lrf",
        decode_errs,
        lax.all_to_all(decoded[None], ROW, split_axis=2, concat_axis=0, tiled=True).astype(
            jnp.float32
        ),
    )
    squares = one_axis_at_a_time(jnp.sum(grad * grad), ROW_COL)
    factor = jnp.minimum(1.0, jnp.sqrt(jnp.float32(FF * D)) / jnp.sqrt(squares + 1e-06))
    return grad * factor


def solution(mesh):
    finer = Mesh(mesh.devices.reshape(8, 2, 4, 8), ("row_0", "row_1", "col_0", "col_1"))
    in_specs = (P(ROW, COL), P(COL, ROW), P(), P(), P())
    out_specs = P(None, COL, ROW)
    return jax.shard_map(
        shards, mesh=finer, in_specs=in_specs, out_specs=out_specs, check_vma=False
    )
```

profile of v0, /device:TPU:8, one launch (start us, length us, event | category | flops | bytes accessed | tf_op | source)
XLA Modules:
  0.0 509.3 jit_solution(16859528297942924830)
XLA Ops:
  0.0 1.9 broadcast_in_dim.19
  1.9 13.2 %all-to-all-start.1 = ((bf16[32,16,924]{2,1,0:T(8,128)(2,1)}), bf16[32,16,924]{2,1,0:T(8,128)(2,1)S(1)}, u32[]{:S(2)}, u32[]{:S(2)}) async-start(bf16[32,16,924]{2,1,0:T(8,128)(2,1)} %broadcast_in_dim.19), calls=%async_computation.1 | async-start | bytes 2097152 | tf_op jit(solution)/shard_map/all_to_all | solution.py:16
  15.8 1.2 divide_reduce_fusion.1
  17.0 1.2 multiply_divide_fusion.1
  18.3 16.3 %all_gather.6 = bf16[8,4096]{1,0:T(8,128)(2,1)S(1)} all-gather(bf16[8,256]{1,0:T(8,128)(2,1)S(1)} %copy-done.1), channel_id=1, replica_groups=mesh['row_0'=8,'row_1'=2,'col_0'=4,'col_1'=8] {'row_0','row_1'}, dimensions={1}, use_global_device_ids=true | all-gather | bytes 69632 | tf_op jit(solution)/shard_map/all_gather | solution.py:85
  34.6 9.4 %while.28 = (s32[]{:T(128)}, f32[8,512]{1,0:T(8,128)S(1)}, f32[8]{0:T(128)S(1)}, bf16[8,4096]{1,0:T(8,128)(2,1)S(1)}, s32[]{:T(128)}, /*index=5*/s32[]{:T(128)}, s32[]{:T(128)}, s32[]{:T(128)}) while((s32[]{:T(128)}, f32[8,512]{1,0:T(8,128)S(1)}, f32[8]{0:T(128)S(1)}, bf16[8,4096]{1,0:T(8,128)(2,1)S(1)}, s32[]{:T(128)}, ...), condition=%wide.region_4.5_spmd.clone, body=%wide.region_3.4_spmd.clone.sunk | while | flops 16391 | bytes 41121 | solution.py:63
  46.2 1.3 divide_reduce_fusion
  47.5 1.3 multiply_divide_fusion
  49.5 9.8 %all-to-all-start = ((bf16[32,8,512]{2,1,0:T(8,128)(2,1)}), bf16[32,8,512]{2,1,0:T(8,128)(2,1)S(1)}, u32[]{:S(2)}, u32[]{:S(2)}) async-start(bf16[32,8,512]{2,1,0:T(8,128)(2,1)} %broadcast_in_dim.16), calls=%async_computation | async-start | bytes 524288 | tf_op jit(solution)/shard_map/all_to_all | solution.py:16
  59.9 1.3 reshape.108
  61.1 23.7 %while.29 = (s32[]{:T(128)}, f32[16,1848]{1,0:T(8,128)S(1)}, f32[16]{0:T(128)S(1)}, bf16[16,29568]{1,0:T(8,128)(2,1)S(1)}, s32[]{:T(128)}, /*index=5*/s32[]{:T(128)}, s32[]{:T(128)}, s32[]{:T(128)}) while((s32[]{:T(128)}, f32[16,1848]{1,0:T(8,128)S(1)}, f32[16]{0:T(128)S(1)}, bf16[16,29568]{1,0:T(8,128)(2,1)S(1)}, s32[]{:T(128)}, ...), condition=%wide.region_7.8_spmd.clone, body=%wide.region_6.7_spmd.clone.sunk | while | flops 118279 | bytes 295841 | solution.py:63
  84.9 18.8 %all_gather.7 = bf16[256,1848]{1,0:T(8,128)(2,1)S(1)} all-gather(bf16[16,1848]{1,0:T(8,128)(2,1)S(1)} %convert_element_type.115), channel_id=1, replica_groups=mesh['row_0'=8,'row_1'=2,'col_0'=4,'col_1'=8] {'row_0','row_1'}, dimensions={0}, use_global_device_ids=true | all-gather | bytes 1005312 | tf_op jit(solution)/shard_map/all_gather | solution.py:92
  104.4 6.8 %copy.23 = bf16[1,512,1848]{2,0,1:T(2,128)(2,1)} copy(bf16[1,512,1848]{1,2,0:T(8,128)(2,1)S(1)} %fusion) | data formatting | bytes 3784704 | tf_op jit(solution)/shard_map/broadcast_in_dim | solution.py:103
  111.7 12.9 %reduce.2 = bf16[512,1848]{1,0:T(8,128)(2,1)S(1)} reduce(bf16[512,1,1848]{2,1,0:T(2,128)(2,1)} %bitcast.43, bf16[]{:T(256)} %broadcast.315), dimensions={1}, to_apply=%bitcast.26.reduce_sub_computation | reduce | bytes 3784706
  124.6 4.5 reshape.111
  129.1 10.0 %all-to-all-start.2 = ((bf16[32,2,14784]{2,1,0:T(2,128)(2,1)}), bf16[32,2,14784]{2,1,0:T(2,128)(2,1)S(1)}, u32[]{:S(2)}, u32[]{:S(2)}) async-start(bf16[32,2,14784]{2,1,0:T(2,128)(2,1)} %reshape.111), calls=%async_computation.2 | async-start | bytes 3801088 | tf_op jit(solution)/shard_map/all_to_all | solution.py:103
  139.3 46.1 %all-to-all-done.2 = bf16[32,2,14784]{2,1,0:T(2,128)(2,1)S(1)} async-done(((bf16[32,2,14784]{2,1,0:T(2,128)(2,1)}), bf16[32,2,14784]{2,1,0:T(2,128)(2,1)S(1)}, u32[]{:S(2)}, u32[]{:S(2)}) %all-to-all-start.2) | async-done | bytes 1892384 | tf_op jit(solution)/shard_map/all_to_all | solution.py:103
  185.4 7.4 %reshape.112 = bf16[512,1,1848]{2,1,0:T(2,128)(2,1)} reshape(bf16[32,2,14784]{2,1,0:T(2,128)(2,1)S(1)} %all-to-all-done.2) | data formatting | bytes 3784704
  192.8 2.4 copy.28
  196.7 22.8 %copy.25 = bf16[1,16,29568]{1,0,2:T(2,128)(2,1)} copy(bf16[1,16,29568]{2,1,0:T(8,128)(2,1)S(1)} %broadcast_in_dim_reshape.3) | data formatting | bytes 1892352 | tf_op jit(solution)/shard_map/broadcast_in_dim;reshape | solution.py:115
  219.5 162.1 %reduce.3 = bf16[29568,16]{1,0:T(8,128)(2,1)} reduce(bf16[29568,1,16]{2,1,0:T(2,128)(2,1)} %bitcast.41, bf16[]{:T(256)} %broadcast.315), dimensions={1}, to_apply=%bitcast.28.reduce_sub_computation | reduce | bytes 1892354
  381.6 10.5 %reshape.113 = bf16[16,2,14784]{2,1,0:T(2,128)(2,1)} reshape(bf16[29568,16]{1,0:T(8,128)(2,1)} %reduce.3) | data formatting | bytes 1892352
  392.1 5.5 %all-to-all-start.3 = ((bf16[16,2,14784]{2,1,0:T(2,128)(2,1)}), bf16[16,2,14784]{2,1,0:T(2,128)(2,1)S(1)}, u32[]{:S(2)}, u32[]{:S(2)}) async-start(bf16[16,2,14784]{2,1,0:T(2,128)(2,1)} %reshape.113), calls=%async_computation.3 | async-start | bytes 1900544 | tf_op jit(solution)/shard_map/all_to_all | solution.py:115
  398.1 22.2 %all-to-all-done.3 = bf16[16,2,14784]{2,1,0:T(2,128)(2,1)S(1)} async-done(((bf16[16,2,14784]{2,1,0:T(2,128)(2,1)}), bf16[16,2,14784]{2,1,0:T(2,128)(2,1)S(1)}, u32[]{:S(2)}, u32[]{:S(2)}) %all-to-all-start.3) | async-done | bytes 946208 | tf_op jit(solution)/shard_map/all_to_all | solution.py:115
  420.3 11.2 %reshape.114 = bf16[29568,1,16]{2,1,0:T(2,128)(2,1)} reshape(bf16[16,2,14784]{2,1,0:T(2,128)(2,1)S(1)} %all-to-all-done.3) | data formatting | bytes 1892352
  431.5 27.1 %copy.26 = bf16[1,16,29568]{2,1,0:T(8,128)(2,1)S(1)} copy(bf16[1,16,29568]{1,0,2:T(2,128)(2,1)} %bitcast.42) | data formatting | bytes 1892352 | tf_op jit(solution)/shard_map/all_to_all | solution.py:115
  458.6 1.6 all_to_all.33
  461.3 16.6 %psum.28 = f32[]{:T(128)} all-reduce(f32[]{:T(128)} %get-tuple-element.211), channel_id=1, replica_groups=mesh['row_0'=8,'row_1'=2,'col_0'=4,'col_1'=8] {'row_0'}, use_global_device_ids=true, to_apply=%region_11.12 | all-reduce | flops 1 | bytes 8 | tf_op jit(solution)/shard_map/psum | solution.py:34
  477.9 3.1 psum.29
  481.0 9.2 %psum.30 = f32[]{:T(128)} all-reduce(f32[]{:T(128)} %psum.29), channel_id=1, replica_groups=mesh['row_0'=8,'row_1'=2,'col_0'=4,'col_1'=8] {'col_0'}, use_global_device_ids=true, to_apply=%region_13.14 | all-reduce | flops 1 | bytes 8 | tf_op jit(solution)/shard_map/psum | solution.py:34
  490.1 17.3 %psum.31 = f32[]{:T(128)} all-reduce(f32[]{:T(128)} %psum.30), channel_id=1, replica_groups=mesh['row_0'=8,'row_1'=2,'col_0'=4,'col_1'=8] {'col_1'}, use_global_device_ids=true, to_apply=%region_14.15 | all-reduce | flops 1 | bytes 8 | tf_op jit(solution)/shard_map/psum | solution.py:34
  508.2 1.1 copy.27
  (80 shorter events, 41.1 us)
Async XLA Ops:
  0.0 15.1 %copy-start.2 = (s32[16]{0:T(128)S(1)}, s32[16]{0:T(128)}, u32[]{:S(2)}) copy-start(s32[16]{0:T(128)} %param.12) | copy-start | bytes 196
  0.0 18.2 %copy-start.1 = (bf16[8,256]{1,0:T(8,128)(2,1)S(1)}, bf16[8,256]{1,0:T(8,128)(2,1)}, u32[]{:S(2)}) copy-start(bf16[8,256]{1,0:T(8,128)(2,1)} %param.10) | copy-start | bytes 12292
  0.0 44.7 %copy-start = (s32[32]{0:T(128)S(1)}, s32[32]{0:T(128)}, u32[]{:S(2)}) copy-start(s32[32]{0:T(128)} %param.11) | copy-start | bytes 388
  1.9 46.9 %all-to-all-start.1 = ((bf16[32,16,924]{2,1,0:T(8,128)(2,1)}), bf16[32,16,924]{2,1,0:T(8,128)(2,1)S(1)}, u32[]{:S(2)}, u32[]{:S(2)}) async-start(bf16[32,16,924]{2,1,0:T(8,128)(2,1)} %broadcast_in_dim.19), calls=%async_computation.1 | async-start | bytes 2097152 | tf_op jit(solution)/shard_map/all_to_all | solution.py:16
  49.5 54.2 %all-to-all-start = ((bf16[32,8,512]{2,1,0:T(8,128)(2,1)}), bf16[32,8,512]{2,1,0:T(8,128)(2,1)S(1)}, u32[]{:S(2)}, u32[]{:S(2)}) async-start(bf16[32,8,512]{2,1,0:T(8,128)(2,1)} %broadcast_in_dim.16), calls=%async_computation | async-start | bytes 524288 | tf_op jit(solution)/shard_map/all_to_all | solution.py:16
  129.1 56.3 %all-to-all-start.2 = ((bf16[32,2,14784]{2,1,0:T(2,128)(2,1)}), bf16[32,2,14784]{2,1,0:T(2,128)(2,1)S(1)}, u32[]{:S(2)}, u32[]{:S(2)}) async-start(bf16[32,2,14784]{2,1,0:T(2,128)(2,1)} %reshape.111), calls=%async_computation.2 | async-start | bytes 3801088 | tf_op jit(solution)/shard_map/all_to_all | solution.py:103
  392.1 28.2 %all-to-all-start.3 = ((bf16[16,2,14784]{2,1,0:T(2,128)(2,1)}), bf16[16,2,14784]{2,1,0:T(2,128)(2,1)S(1)}, u32[]{:S(2)}, u32[]{:S(2)}) async-start(bf16[16,2,14784]{2,1,0:T(2,128)(2,1)} %reshape.113), calls=%async_computation.3 | async-start | bytes 1900544 | tf_op jit(solution)/shard_map/all_to_all | solution.py:115
where the time goes:
time: 511 us; the launch traced here: 509 us
  other arithmetic  199 us (39%)
  local copies, waits for them, and re-layouts  118 us (23%)
  blocking collectives  81.3 us (16%)
  waiting for transfers between devices  68.3 us (13%)
  starting transfers between devices  38.5 us (8%)
    unnamed x4, other arithmetic  175 us
    psum x4, blocking collectives, one_axis_at_a_time(): shard = lax.psum(shard, axis)  46.1 us
    all_to_all x1, waiting for transfers between devices, shards(): lax.all_to_all(product[None], COL, split_axis=1, concat_axis=0, tiled=True)  46.1 us
    unnamed x12, local copies, waits for them, and re-layouts  36.5 us
    all_to_all x2, local copies, waits for them, and re-layouts, shards(): lax.all_to_all(decoded[None], ROW, split_axis=2, concat_axis=0, tiled=True)  28.6 us
    another operation x2, local copies, waits for them, and re-layouts, shards(): decoded[None]  23.8 us
    all_to_all x2, starting transfers between devices, copy_for_each(): lax.all_to_all(jnp.broadcast_to(shard[None], (peers, *shard.shape)), axis...  22.9 us
    all_to_all x1, waiting for transfers between devices, shards(): lax.all_to_all(decoded[None], ROW, split_axis=2, concat_axis=0, tiled=True)  22.2 us
  transfers between devices with their start and end apart: 4, of which 2 were waited for; matrix products, arithmetic and copies ran while one was open for 8% of the time, Pallas kernels for 0%

commit v1 on v0

--- a/solution.py
+++ b/solution.py
@@ -1,3 +1,4 @@
+import functools
 import jax
 import jax.numpy as jnp
 from jax import lax
@@ -9,6 +10,15 @@
 COL = ("col_0", "col_1")
 ROW = ("row_0", "row_1")
 ROW_COL = ("row_0", "row_1", "col_0", "col_1")
+
+
+def boxes_write(z_in, axis_id):
+    w1 = jnp.stack(jnp.split(z_in, jax.lax.axis_size(axis_id), axis=2))
+    next_value = jax.lax.all_to_all(w1, axis_id, 0, 0)
+    return jnp.concatenate(next_value, axis=0)
+
+
+edit_series_all_up = functools.partial(boxes_write, axis_id=ROW)
 
 
 def copy_for_each(shard, axis):
@@ -110,11 +120,7 @@
         work_errs, rank_signs(row_points, all_rows), jnp.ones((row_count,), jnp.float32), data_errs
     )
     grad = jnp.einsum(
-        "il,irf->lrf",
-        decode_errs,
-        lax.all_to_all(decoded[None], ROW, split_axis=2, concat_axis=0, tiled=True).astype(
-            jnp.float32
-        ),
+        "il,irf->lrf", decode_errs, edit_series_all_up(decoded[None]).astype(jnp.float32)
     )
     squares = one_axis_at_a_time(jnp.sum(grad * grad), ROW_COL)
     factor = jnp.minimum(1.0, jnp.sqrt(jnp.float32(FF * D)) / jnp.sqrt(squares + 1e-06))

time: 511 us -> 287 us (0.56)
  other arithmetic: 199 us -> 36.8 us
  local copies, waits for them, and re-layouts: 118 us -> 56.7 us
    unnamed x4 -> x3, other arithmetic: 175 us -> 12.9 us
    all_to_all x2 -> x0, local copies, waits for them, and re-layouts: 28.6 us -> none  [shards(): lax.all_to_all(decoded[None], ROW, split_axis=2, concat_axis=0, tiled=True)]
    another operation x2 -> x1, local copies, waits for them, and re-layouts: 23.8 us -> 1 us  [shards(): decoded[None]]
    unnamed x12 -> x25, local copies, waits for them, and re-layouts: 36.5 us -> 25.4 us
  transfers between devices with their start and end apart: 4 -> 4, of which waited for: 2 -> 2; matrix products, arithmetic and copies ran while one was open for 8% -> 15% of each run, Pallas kernels for 0% -> 0%
where the time goes in v1:
time: 287 us; the launch traced here: 286 us
  blocking collectives  81.4 us (28%)
  waiting for transfers between devices  69.2 us (24%)
  local copies, waits for them, and re-layouts  56.7 us (20%)
  starting transfers between devices  38.3 us (13%)
  other arithmetic  36.8 us (13%)
    all_to_all x1, waiting for transfers between devices, shards(): lax.all_to_all(product[None], COL, split_axis=1, concat_axis=0, tiled=True)  46.3 us
    psum x4, blocking collectives, one_axis_at_a_time(): shard = lax.psum(shard, axis)  46.3 us
    unnamed x25, local copies, waits for them, and re-layouts  25.4 us
    all_to_all x2, starting transfers between devices, copy_for_each(): lax.all_to_all(jnp.broadcast_to(shard[None], (peers, *shard.shape)), axis...  22.9 us
    all_to_all x1, waiting for transfers between devices, boxes_write(): next_value = jax.lax.all_to_all(w1, axis_id, 0, 0)  22.9 us
    all_gather x1, blocking collectives, shards(): lax.all_gather(coded_acts, ROW, axis=0, tiled=True)  18.8 us
    add x24, other arithmetic, add_block(): return total + factor * piece  17.1 us
    all_gather x1, blocking collectives, shards(): full_errs = lax.all_gather(output_errors, ROW, axis=1, tiled=True)  16.3 us
  transfers between devices with their start and end apart: 4, of which 2 were waited for; matrix products, arithmetic and copies ran while one was open for 15% of the time, Pallas kernels for 0%

profile of v1, /device:TPU:8, one launch (start us, length us, event | category | flops | bytes accessed | tf_op | source)
XLA Modules:
  0.0 286.2 jit_solution(11174596957337147805)
XLA Ops:
  0.0 1.9 broadcast_in_dim.19
  1.9 13.2 %all-to-all-start.1 = ((bf16[32,16,924]{2,1,0:T(8,128)(2,1)}), bf16[32,16,924]{2,1,0:T(8,128)(2,1)S(1)}, u32[]{:S(2)}, u32[]{:S(2)}) async-start(bf16[32,16,924]{2,1,0:T(8,128)(2,1)} %broadcast_in_dim.19), calls=%async_computation.1 | async-start | bytes 2097152 | tf_op jit(solution)/shard_map/all_to_all | solution.py:26
  15.8 1.2 divide_reduce_fusion.1
  17.0 1.2 multiply_divide_fusion.1
  18.3 16.3 %all_gather.6 = bf16[8,4096]{1,0:T(8,128)(2,1)S(1)} all-gather(bf16[8,256]{1,0:T(8,128)(2,1)S(1)} %copy-done.1), channel_id=1, replica_groups=mesh['row_0'=8,'row_1'=2,'col_0'=4,'col_1'=8] {'row_0','row_1'}, dimensions={1}, use_global_device_ids=true | all-gather | bytes 69632 | tf_op jit(solution)/shard_map/all_gather | solution.py:95
  34.6 9.4 %while.28 = (s32[]{:T(128)}, f32[8,512]{1,0:T(8,128)S(1)}, f32[8]{0:T(128)S(1)}, bf16[8,4096]{1,0:T(8,128)(2,1)S(1)}, s32[]{:T(128)}, /*index=5*/s32[]{:T(128)}, s32[]{:T(128)}, s32[]{:T(128)}) while((s32[]{:T(128)}, f32[8,512]{1,0:T(8,128)S(1)}, f32[8]{0:T(128)S(1)}, bf16[8,4096]{1,0:T(8,128)(2,1)S(1)}, s32[]{:T(128)}, ...), condition=%wide.region_4.5_spmd.clone, body=%wide.region_3.4_spmd.clone.sunk | while | flops 16391 | bytes 41121 | solution.py:73
  46.2 1.3 divide_reduce_fusion
  47.5 1.3 multiply_divide_fusion
  49.5 9.8 %all-to-all-start = ((bf16[32,8,512]{2,1,0:T(8,128)(2,1)}), bf16[32,8,512]{2,1,0:T(8,128)(2,1)S(1)}, u32[]{:S(2)}, u32[]{:S(2)}) async-start(bf16[32,8,512]{2,1,0:T(8,128)(2,1)} %broadcast_in_dim.16), calls=%async_computation | async-start | bytes 524288 | tf_op jit(solution)/shard_map/all_to_all | solution.py:26
  59.9 1.3 reshape.111
  61.1 23.7 %while.29 = (s32[]{:T(128)}, f32[16,1848]{1,0:T(8,128)S(1)}, f32[16]{0:T(128)S(1)}, bf16[16,29568]{1,0:T(8,128)(2,1)S(1)}, s32[]{:T(128)}, /*index=5*/s32[]{:T(128)}, s32[]{:T(128)}, s32[]{:T(128)}) while((s32[]{:T(128)}, f32[16,1848]{1,0:T(8,128)S(1)}, f32[16]{0:T(128)S(1)}, bf16[16,29568]{1,0:T(8,128)(2,1)S(1)}, s32[]{:T(128)}, ...), condition=%wide.region_7.8_spmd.clone, body=%wide.region_6.7_spmd.clone.sunk | while | flops 118279 | bytes 295841 | solution.py:73
  63.3 0.8 select_add_fusion.5
  64.8 0.8 select_add_fusion.5
  67.8 0.8 select_add_fusion.5
  69.2 0.8 select_add_fusion.5
  84.9 18.8 %all_gather.7 = bf16[256,1848]{1,0:T(8,128)(2,1)S(1)} all-gather(bf16[16,1848]{1,0:T(8,128)(2,1)S(1)} %convert_element_type.115), channel_id=1, replica_groups=mesh['row_0'=8,'row_1'=2,'col_0'=4,'col_1'=8] {'row_0','row_1'}, dimensions={0}, use_global_device_ids=true | all-gather | bytes 1005312 | tf_op jit(solution)/shard_map/all_gather | solution.py:102
  104.4 6.8 %copy.322 = bf16[1,512,1848]{2,0,1:T(2,128)(2,1)} copy(bf16[1,512,1848]{1,2,0:T(8,128)(2,1)S(1)} %fusion) | data formatting | bytes 3784704 | tf_op jit(solution)/shard_map/broadcast_in_dim | solution.py:113
  111.7 12.9 %reduce.2 = bf16[512,1848]{1,0:T(8,128)(2,1)S(1)} reduce(bf16[512,1,1848]{2,1,0:T(2,128)(2,1)} %bitcast.101, bf16[]{:T(256)} %broadcast.315), dimensions={1}, to_apply=%bitcast.88.reduce_sub_computation | reduce | bytes 3784706
  124.6 4.5 %reshape.115 = bf16[32,2,14784]{2,1,0:T(2,128)(2,1)} reshape(bf16[512,1848]{1,0:T(8,128)(2,1)S(1)} %reduce.2) | data formatting | bytes 3784704
  129.1 9.8 %all-to-all-start.2 = ((bf16[32,2,14784]{2,1,0:T(2,128)(2,1)}), bf16[32,2,14784]{2,1,0:T(2,128)(2,1)S(1)}, u32[]{:S(2)}, u32[]{:S(2)}) async-start(bf16[32,2,14784]{2,1,0:T(2,128)(2,1)} %reshape.115), calls=%async_computation.2 | async-start | bytes 3801088 | tf_op jit(solution)/shard_map/all_to_all | solution.py:113
  139.1 46.3 %all-to-all-done.2 = bf16[32,2,14784]{2,1,0:T(2,128)(2,1)S(1)} async-done(((bf16[32,2,14784]{2,1,0:T(2,128)(2,1)}), bf16[32,2,14784]{2,1,0:T(2,128)(2,1)S(1)}, u32[]{:S(2)}, u32[]{:S(2)}) %all-to-all-start.2) | async-done | bytes 1892384 | tf_op jit(solution)/shard_map/all_to_all | solution.py:113
  185.4 7.4 %reshape.116 = bf16[512,1,1848]{2,1,0:T(2,128)(2,1)} reshape(bf16[32,2,14784]{2,1,0:T(2,128)(2,1)S(1)} %all-to-all-done.2) | data formatting | bytes 3784704
  192.8 2.4 copy.326
  195.7 1.0 broadcast_in_dim_reshape.3
  208.0 5.6 %all-to-all-start.3 = ((bf16[16,1,16,1848]{3,2,1,0:T(8,128)(2,1)}), bf16[16,1,16,1848]{3,2,1,0:T(8,128)(2,1)S(1)}, u32[]{:S(2)}, u32[]{:S(2)}) async-start(bf16[16,1,16,1848]{3,2,1,0:T(8,128)(2,1)} %fusion.7), calls=%async_computation.3 | async-start | bytes 1966080 | tf_op jit(solution)/shard_map/all_to_all | solution.py:17
  214.0 22.9 %all-to-all-done.3 = bf16[16,1,16,1848]{3,2,1,0:T(8,128)(2,1)S(1)} async-done(((bf16[16,1,16,1848]{3,2,1,0:T(8,128)(2,1)}), bf16[16,1,16,1848]{3,2,1,0:T(8,128)(2,1)S(1)}, u32[]{:S(2)}, u32[]{:S(2)}) %all-to-all-start.3) | async-done | bytes 946208 | tf_op jit(solution)/shard_map/all_to_all | solution.py:17
  236.9 1.1 multiply_reduce_fusion
  238.0 16.7 %psum.28 = f32[]{:T(128)} all-reduce(f32[]{:T(128)} %get-tuple-element.211), channel_id=1, replica_groups=mesh['row_0'=8,'row_1'=2,'col_0'=4,'col_1'=8] {'row_0'}, use_global_device_ids=true, to_apply=%region_11.12 | all-reduce | flops 1 | bytes 8 | tf_op jit(solution)/shard_map/psum | solution.py:44
  254.8 3.1 %psum.29 = f32[]{:T(128)} all-reduce(f32[]{:T(128)} %psum.28), channel_id=1, replica_groups=mesh['row_0'=8,'row_1'=2,'col_0'=4,'col_1'=8] {'row_1'}, use_global_device_ids=true, to_apply=%region_12.13 | all-reduce | flops 1 | bytes 8 | tf_op jit(solution)/shard_map/psum | solution.py:44
  257.8 9.1 %psum.30 = f32[]{:T(128)} all-reduce(f32[]{:T(128)} %psum.29), channel_id=1, replica_groups=mesh['row_0'=8,'row_1'=2,'col_0'=4,'col_1'=8] {'col_0'}, use_global_device_ids=true, to_apply=%region_13.14 | all-reduce | flops 1 | bytes 8 | tf_op jit(solution)/shard_map/psum | solution.py:44
  267.0 17.3 %psum.31 = f32[]{:T(128)} all-reduce(f32[]{:T(128)} %psum.30), channel_id=1, replica_groups=mesh['row_0'=8,'row_1'=2,'col_0'=4,'col_1'=8] {'col_1'}, use_global_device_ids=true, to_apply=%region_14.15 | all-reduce | flops 1 | bytes 8 | tf_op jit(solution)/shard_map/psum | solution.py:44
  285.1 1.1 copy.325
  (90 shorter events, 47.3 us)
Async XLA Ops:
  0.0 15.1 %copy-start.2 = (s32[16]{0:T(128)S(1)}, s32[16]{0:T(128)}, u32[]{:S(2)}) copy-start(s32[16]{0:T(128)} %param.12) | copy-start | bytes 196
  0.0 18.2 %copy-start.1 = (bf16[8,256]{1,0:T(8,128)(2,1)S(1)}, bf16[8,256]{1,0:T(8,128)(2,1)}, u32[]{:S(2)}) copy-start(bf16[8,256]{1,0:T(8,128)(2,1)} %param.10) | copy-start | bytes 12292
  0.0 44.7 %copy-start = (s32[32]{0:T(128)S(1)}, s32[32]{0:T(128)}, u32[]{:S(2)}) copy-start(s32[32]{0:T(128)} %param.11) | copy-start | bytes 388
  1.9 46.9 %all-to-all-start.1 = ((bf16[32,16,924]{2,1,0:T(8,128)(2,1)}), bf16[32,16,924]{2,1,0:T(8,128)(2,1)S(1)}, u32[]{:S(2)}, u32[]{:S(2)}) async-start(bf16[32,16,924]{2,1,0:T(8,128)(2,1)} %broadcast_in_dim.19), calls=%async_computation.1 | async-start | bytes 2097152 | tf_op jit(solution)/shard_map/all_to_all | solution.py:26
  49.5 54.2 %all-to-all-start = ((bf16[32,8,512]{2,1,0:T(8,128)(2,1)}), bf16[32,8,512]{2,1,0:T(8,128)(2,1)S(1)}, u32[]{:S(2)}, u32[]{:S(2)}) async-start(bf16[32,8,512]{2,1,0:T(8,128)(2,1)} %broadcast_in_dim.16), calls=%async_computation | async-start | bytes 524288 | tf_op jit(solution)/shard_map/all_to_all | solution.py:26
  129.1 56.3 %all-to-all-start.2 = ((bf16[32,2,14784]{2,1,0:T(2,128)(2,1)}), bf16[32,2,14784]{2,1,0:T(2,128)(2,1)S(1)}, u32[]{:S(2)}, u32[]{:S(2)}) async-start(bf16[32,2,14784]{2,1,0:T(2,128)(2,1)} %reshape.115), calls=%async_computation.2 | async-start | bytes 3801088 | tf_op jit(solution)/shard_map/all_to_all | solution.py:113
  208.0 28.9 %all-to-all-start.3 = ((bf16[16,1,16,1848]{3,2,1,0:T(8,128)(2,1)}), bf16[16,1,16,1848]{3,2,1,0:T(8,128)(2,1)S(1)}, u32[]{:S(2)}, u32[]{:S(2)}) async-start(bf16[16,1,16,1848]{3,2,1,0:T(8,128)(2,1)} %fusion.7), calls=%async_computation.3 | async-start | bytes 1966080 | tf_op jit(solution)/shard_map/all_to_all | solution.py:17
